TPU v7x, 512 devices: a whole 4x4x16 slice. The times are simulated.
512 devices in a mesh: qa: 16 (over z_hi, y, core), qb: 32 (over x, z_lo).
Axes of the slice: x: 4, y: 4, z: 16 (z_hi: 2, z_lo: 8; z = z_hi * 8 + z_lo), core: 2. Of those that a mesh axis runs over, the one named last changes fastest.
Arguments:
- amplitudes: float32 [16, 32, 16, 128, 128], P('qa', 'qb'), may hold values from -6 to 6
- angles: float32 [2, 23], replicated, may hold values from -3.140625 to 3.140625
- hadamard: int32 [2, 23], replicated, may hold values 0 or 1
- cz_pairs: int32 [2, 14, 2], replicated, may hold values from 0 to 26, as said below
Outputs:
- final_state: float32 [16, 32, 16, 128, 128], P('qa', 'qb')
Inputs may be any that keep to these rules, and one draw needn't show every extreme that they name: `cz_pairs`: the two qubits of a pair differ; in each layer the pairs are a random matching of all 27 qubits, and when 27 is odd one qubit is in two pairs.
All inputs are finite; a program needn't handle non-finite values.
Results may differ from a plain program's by a relative error of at most 0.00013.
Values sent between devices are 32-bit elements; how exact they have to be, the bound alone decides.
A program may use at most 64 MiB of HBM per device.

v0:
```python
import functools
import math

import jax
import jax.numpy as jnp
from jax import lax
from jax.experimental import pallas as pl
from jax.experimental.pallas import tpu as pltpu
from jax.sharding import PartitionSpec as P

MESH = pl.DeviceIdType.MESH
F32 = jnp.float32
BF16 = jnp.bfloat16

Z_HALVES = 2
X_CHIPS = 4


def gate_entries(angles, hadamard):
    layers, count = angles.shape
    shape = (layers, 4, count)
    entry = lax.broadcasted_iota(jnp.int32, shape, 1)
    angle = jnp.broadcast_to(angles[:, None, :], shape)
    weight = jnp.broadcast_to(hadamard[:, None, :], shape).astype(F32)
    cos_part, sin_part = jnp.cos(angle), jnp.sin(angle)
    root = math.sqrt(0.5)
    upper = entry < 2
    left = entry % 2 == 0
    near = jnp.where(upper, cos_part, sin_part)
    far = jnp.where(upper, -sin_part, cos_part)
    mix_near = jnp.where(left, 1.0 - weight + weight * root, weight * root)
    mix_far = jnp.where(left, weight * root, 1.0 - weight - weight * root)
    return near * mix_near + far * mix_far


def split(value):
    high = value.astype(BF16)
    return high, (value - high.astype(F32)).astype(BF16)


def dot3(left, right):
    dot = functools.partial(jnp.dot, preferred_element_type=F32)
    return dot(left[0], right[0]) + (dot(left[0], right[1]) + dot(left[1], right[0]))


def log2(value):
    return value.bit_length() - 1


def kernel(
    sizes,
    gates, pairs, amp, out,
    send_z, recv_z, send_p, recv_p, send_b, recv_b,
    gk, gm, gab, sign_mid, sign_end, mid, send_sem, recv_sem,
):
    zh, zl, xc, yc, halves, ex, kk = sizes
    nz, np_, nb, na = zh * zl, xc * yc, xc * zl, zh * yc
    mm = halves * zl * ex * xc
    nab = na * nb
    bits_a, bits_b, bits_x, bits_m, bits_k = log2(na), log2(nb), log2(na), log2(mm), log2(kk)
    qubits = bits_a + bits_b + bits_x + bits_m + bits_k
    shift_m = bits_k
    shift_x = shift_m + bits_m
    shift_b = shift_x + bits_x
    shift_a = shift_b + bits_b
    rot_m = bits_a + bits_b
    rot_k = rot_m + bits_m
    rows_p = ex * zh * zl
    rows_b = ex * na
    sub = ex * xc

    me_a, me_b = lax.axis_index("qa"), lax.axis_index("qb")
    my_zh, my_yc = lax.div(me_a, yc), lax.rem(me_a, yc)
    my_x, my_zl = lax.div(me_b, zl), lax.rem(me_b, zl)
    my_z = my_zh * zl + my_zl
    my_p = my_x * yc + my_yc

    def either_way(step, count):
        odd = lax.rem(step, 2)
        half = lax.div(step + 1, 2)
        return odd * half + (1 - odd) * (count - half)

    def at_z(step):
        z = lax.rem(my_z + either_way(step, nz), nz)
        return z, (lax.div(z, zl) * yc + my_yc, my_x * zl + lax.rem(z, zl))

    def at_p(step):
        p = lax.rem(my_p + step, np_)
        return p, (my_zh * yc + lax.rem(p, yc), lax.div(p, yc) * zl + my_zl)

    def at_b(step):
        b = lax.rem(my_b_start + step, nb)
        return b, (me_a, b)

    my_b_start = me_b

    barrier = pltpu.get_barrier_semaphore()
    for place, count in ((at_z, nz), (at_p, np_), (at_b, nb)):
        @pl.loop(1, count)
        def _(step, place=place):
            pl.semaphore_signal(barrier, inc=1, device_id=place(step)[1], device_id_type=MESH)

    def entry(layer, qubit, out_one, in_one):
        value = lambda number: gates[layer, number, qubit]
        return jnp.where(
            out_one,
            jnp.where(in_one, value(3), value(2)),
            jnp.where(in_one, value(1), value(0)),
        )

    def matrix(layer, out_index, in_index, qubits_and_bits):
        result = None
        for qubit, out_bit, in_bit in qubits_and_bits:
            factor = entry(
                layer, qubit, (out_index & (1 << out_bit)) != 0, (in_index & (1 << in_bit)) != 0
            )
            result = factor if result is None else result * factor
        return result

    def signs(layer, index):
        odd = jnp.zeros(index.shape, jnp.int32)
        for pair in range(pairs.shape[1]):
            mask = jnp.left_shift(1, qubits - 1 - pairs[layer, pair, 0]) | jnp.left_shift(
                1, qubits - 1 - pairs[layer, pair, 1]
            )
            odd = odd ^ jnp.where((index & mask) == mask, 1, 0)
        return 1.0 - 2.0 * odd.astype(F32)

    def build_k(layer):
        rows = lax.broadcasted_iota(jnp.int32, (kk, kk), 0)
        cols = lax.broadcasted_iota(jnp.int32, (kk, kk), 1)
        bits = [(rot_k + n, bits_k - 1 - n, bits_k - 1 - n) for n in range(bits_k)]
        gk[layer, 0], gk[layer, 1] = split(matrix(layer, cols, rows, bits))

    bits_zl, bits_xc, bits_ex, bits_h = log2(zl), log2(xc), log2(ex), log2(halves)

    def build_m(layer):
        rows = lax.broadcasted_iota(jnp.int32, (mm, mm), 0)
        cols = lax.broadcasted_iota(jnp.int32, (mm, mm), 1)
        natural = [bits_m - 1 - n for n in range(bits_m)]
        if layer == 0:
            in_bits = natural
        else:
            in_bits = (
                natural[:bits_h]
                + [bits_zl - 1 - n for n in range(bits_zl)]
                + [bits_zl + bits_xc + bits_ex - 1 - n for n in range(bits_ex)]
                + [bits_zl + bits_xc - 1 - n for n in range(bits_xc)]
            )
        bits = [(rot_m + n, natural[n], in_bits[n]) for n in range(bits_m)]
        gm[layer, 0], gm[layer, 1] = split(matrix(layer, rows, cols, bits))

    bits_yc, bits_zh = log2(yc), log2(zh)

    def mid_bits():
        a_bits = [bits_zl + bits_zh - 1 - n for n in range(bits_zh)]
        a_bits += [bits_zl + bits_zh + bits_yc - 1 - n for n in range(bits_yc)]
        b_bits = [bits_zl + bits_zh + bits_yc + bits_xc - 1 - n for n in range(bits_xc)]
        b_bits += [bits_zl - 1 - n for n in range(bits_zl)]
        return a_bits + b_bits

    tile = min(nab, 64)

    def build_ab(layer):
        mids = mid_bits()
        if layer == 0:
            outs = mids
        else:
            outs = [bits_a - 1 - n for n in range(bits_a)]
            outs += [bits_a + bits_b - 1 - n for n in range(bits_b)]
        bits = [(n, outs[n], mids[n]) for n in range(bits_a + bits_b)]

        @pl.loop(0, nab // tile)
        def _(step):
            start = pl.multiple_of(step * tile, tile)
            rows = lax.broadcasted_iota(jnp.int32, (tile, nab), 0) + start
            cols = lax.broadcasted_iota(jnp.int32, (tile, nab), 1)
            high, low = split(matrix(layer, rows, cols, bits))
            gab[layer, 0, pl.ds(start, tile), :] = high
            gab[layer, 1, pl.ds(start, tile), :] = low

    sign_tile = min(nab, 128)

    def build_sign_mid():
        mids = mid_bits()
        per = nab // sign_tile

        @pl.loop(0, halves * ex * per)
        def _(step):
            part, start = lax.div(step, per), pl.multiple_of(lax.rem(step, per) * sign_tile, sign_tile)
            half, extra = lax.div(part, ex), lax.rem(part, ex)
            rows = lax.broadcasted_iota(jnp.int32, (sign_tile, kk), 0) + start
            cols = lax.broadcasted_iota(jnp.int32, (sign_tile, kk), 1)
            index = cols
            for n in range(bits_a + bits_b):
                index = index | (((rows >> mids[n]) & 1) << (qubits - 1 - n))
            m = ((half * zl + my_zl) * ex + extra) * xc + my_x
            index = index + (m * (1 << shift_m) + me_a * (1 << shift_x))
            sign_mid[half, pl.ds(start, sign_tile), pl.ds(pl.multiple_of(extra * kk, kk), kk)] = signs(0, index)

    def build_sign_end():
        @pl.loop(0, na)
        def _(a):
            rows = lax.broadcasted_iota(jnp.int32, (mm, kk), 0)
            cols = lax.broadcasted_iota(jnp.int32, (mm, kk), 1)
            index = cols + rows * (1 << shift_m)
            index = index + (me_a * (1 << shift_x) + me_b * (1 << shift_b) + a * (1 << shift_a))
            sign_end[a] = signs(1, index)

    build_k(0)
    build_m(0)
    together = 4

    @pl.loop(0, na // together)
    def _(step):
        first = step * together
        block = amp[pl.ds(first, together)].reshape(together * mm, kk)
        block = dot3(split(block), (gk[0, 0], gk[0, 1]))
        matrix_m = (gm[0, 0], gm[0, 1])
        for n in range(together):
            done = dot3(matrix_m, split(block[n * mm : (n + 1) * mm]))
            done = done.reshape(halves, zl, sub, kk)
            x = first + n
            send_z[:, pl.ds(lax.div(x, yc) * zl, zl), lax.rem(x, yc)] = done

    pl.semaphore_wait(barrier, nz + np_ + nb - 3)

    def send_all(stage, half, count, place, mine, source, target):
        @pl.loop(1, count)
        def _(step):
            number, device = place(step)
            pltpu.make_async_remote_copy(
                src_ref=source.at[half, number],
                dst_ref=target.at[half, mine],
                send_sem=send_sem.at[stage, half],
                recv_sem=recv_sem.at[stage, half],
                device_id=device,
                device_id_type=MESH,
            ).start()

        pltpu.make_async_copy(
            source.at[half, mine], target.at[half, mine], recv_sem.at[stage, half]
        ).start()

    def wait_all(stage, half, target):
        pltpu.make_async_copy(target.at[half], target.at[half], recv_sem.at[stage, half]).wait()

    def wait_sent(stage, half, count, source):
        part = source.at[half, pl.ds(0, count - 1)]
        pltpu.make_async_copy(part, part, send_sem.at[stage, half]).wait()

    for half in range(halves):
        send_all(0, half, nz, at_z, my_z, send_z, recv_z)

    build_ab(0)
    build_ab(1)
    build_sign_mid()

    @pl.loop(0, halves)
    def _(half):
        wait_all(0, half, recv_z)

        @pl.loop(0, yc)
        def _(xr):
            for z_half in range(zh):
                for low in range(sub):
                    rows = recv_z[half, pl.ds(z_half * zl, zl), xr, low, :]
                    extra, x = low // xc, low % xc
                    send_p[half, x * yc + xr, pl.ds((extra * zh + z_half) * zl, zl), :] = rows

        send_all(1, half, np_, at_p, my_p, send_p, recv_p)
        wait_all(1, half, recv_p)
        parts = []
        for extra in range(ex):
            part = recv_p[half, :, pl.ds(extra * zh * zl, zh * zl), :]
            parts.append(part.reshape(nab, kk))
        high, low = split(jnp.concatenate(parts, axis=1))
        mid[0, 0] = high
        mid[0, 1] = low
        mid_tile = min(nab, 128)

        @pl.loop(0, nab // mid_tile)
        def _(step):
            start = pl.multiple_of(step * mid_tile, mid_tile)
            left = (gab[0, 0, pl.ds(start, mid_tile), :], gab[0, 1, pl.ds(start, mid_tile), :])
            value = dot3(left, (mid[0, 0], mid[0, 1])) * sign_mid[half, pl.ds(start, mid_tile), :]
            high, low = split(value)
            mid[1, 0, pl.ds(start, mid_tile), :] = high
            mid[1, 1, pl.ds(start, mid_tile), :] = low

        @pl.loop(0, nab // mid_tile)
        def _(step):
            start = pl.multiple_of(step * mid_tile, mid_tile)
            left = (gab[1, 0, pl.ds(start, mid_tile), :], gab[1, 1, pl.ds(start, mid_tile), :])
            value = dot3(left, (mid[1, 0], mid[1, 1]))
            places = mid_tile // na
            for extra in range(ex):
                part = value[:, extra * kk : (extra + 1) * kk].reshape(places, na, kk)
                send_b[half, pl.ds(step * places, places), pl.ds(extra * na, na), :] = part

        send_all(2, half, nb, at_b, me_b, send_b, recv_b)

    build_k(1)
    build_m(1)
    build_sign_end()
    for half in range(halves):
        wait_all(2, half, recv_b)

    @pl.loop(0, na)
    def _(a):
        parts = []
        for half in range(halves):
            for extra in range(ex):
                for x in range(xc):
                    parts.append(recv_b[half, pl.ds(x * zl, zl), extra * na + a, :])
        block = jnp.concatenate(parts, axis=0)
        block = dot3(split(block), (gk[1, 0], gk[1, 1]))
        block = dot3((gm[1, 0], gm[1, 1]), split(block))
        out[a] = block * sign_end[a]

    for half in range(halves):
        wait_sent(0, half, nz, send_z)
        wait_sent(1, half, np_, send_p)
        wait_sent(2, half, nb, send_b)


def per_device(amplitudes, angles, hadamard, cz_pairs):
    count_a, count_b = lax.axis_size("qa"), lax.axis_size("qb")
    x_total, mm, kk = amplitudes.shape[2:]
    zh, xc = Z_HALVES, X_CHIPS
    yc, zl = count_a // zh, count_b // xc
    halves = 2
    ex = mm // (halves * zl * xc)
    sizes = (zh, zl, xc, yc, halves, ex, kk)
    nab = count_a * count_b
    vmem = pl.BlockSpec(memory_space=pltpu.VMEM)
    smem = pl.BlockSpec(memory_space=pltpu.SMEM)
    shape_z = (halves, zh * zl, yc, ex * xc, kk)
    shape_p = (halves, xc * yc, ex * zh * zl, kk)
    shape_b = (halves, xc * zl, ex * count_a, kk)
    result = pl.pallas_call(
        functools.partial(kernel, sizes),
        out_shape=jax.ShapeDtypeStruct((count_a, mm, kk), F32),
        in_specs=[smem, smem, vmem],
        out_specs=vmem,
        scratch_shapes=[
            pltpu.VMEM(shape_z, F32),
            pltpu.VMEM(shape_z, F32),
            pltpu.VMEM(shape_p, F32),
            pltpu.VMEM(shape_p, F32),
            pltpu.VMEM(shape_b, F32),
            pltpu.VMEM(shape_b, F32),
            pltpu.VMEM((2, 2, kk, kk), BF16),
            pltpu.VMEM((2, 2, mm, mm), BF16),
            pltpu.VMEM((2, 2, nab, nab), BF16),
            pltpu.VMEM((halves, nab, ex * kk), F32),
            pltpu.VMEM((count_a, mm, kk), F32),
            pltpu.VMEM((2, 2, nab, ex * kk), BF16),
            pltpu.SemaphoreType.DMA((3, halves)),
            pltpu.SemaphoreType.DMA((3, halves)),
        ],
        compiler_params=pltpu.CompilerParams(
            collective_id=0, has_side_effects=True, vmem_limit_bytes=40 * 2**20
        ),
    )(gate_entries(angles, hadamard), cz_pairs, amplitudes.reshape(x_total, mm, kk))
    return result.reshape(1, 1, count_a, mm, kk)


def solution(mesh):
    return jax.shard_map(
        per_device,
        mesh=mesh,
        in_specs=(P("qa", "qb", None, None, None), P(), P(), P()),
        out_specs=P("qa", "qb", None, None, None),
        check_vma=False,
    )
```

profile of v0, /device:TPU:1, one launch (start us, length us, event | category | flops | bytes accessed | tf_op | source)
XLA Modules:
  0.0 118.6 jit_solution(16392791457329928599)
XLA Ops:
  0.0 0.0 copy-start.3
  0.0 0.0 copy-start.2
  0.0 0.7 copy-done.3
  0.7 0.0 copy-done.2
  0.8 0.0 copy-start.1
  0.8 0.1 multiply_add_fusion.gates
  0.8 0.6 copy-done.1
  1.4 0.1 copy.5.pairs
  1.5 0.0 copy-start
  1.5 1.2 %copy-done = f32[1,1,16,128,128]{4,3,2,1,0:T(8,128)S(1)} copy-done((f32[1,1,16,128,128]{4,3,2,1,0:T(8,128)S(1)}, f32[1,1,16,128,128]{4,3,2,1,0:T(8,128)}, u32[]{:S(2)}) %copy-start) | copy-done | bytes 1048600
  2.8 114.8 %shard_map.46 = f32[16,128,128]{2,1,0:T(8,128)S(1)} custom-call(f32[2,4,23]{2,1,0:T(4,128)S(1)} %multiply_add_fusion.gates, s32[2,14,2]{2,1,0:T(8,128)S(1)} %copy.5.pairs, f32[16,128,128]{2,1,0:T(8,128)S(1)} %bitcast.3), custom_call_target="tpu_custom_call" | custom-call | tf_op jit(solution)/shard_map/pallas_call | solution.py:341
  117.6 1.0 copy.7
  (4 shorter events, 0.1 us)
Async XLA Ops:
  0.0 0.7 copy-start.3
  0.0 0.7 copy-start.2
  0.8 0.7 copy-start.1
  1.5 1.2 %copy-start = (f32[1,1,16,128,128]{4,3,2,1,0:T(8,128)S(1)}, f32[1,1,16,128,128]{4,3,2,1,0:T(8,128)}, u32[]{:S(2)}) copy-start(f32[1,1,16,128,128]{4,3,2,1,0:T(8,128)} %param.4) | copy-start | bytes 3145732
where the time goes:
time: 119 us
  Pallas kernels  115 us (97%)
  local copies, waits for them, and re-layouts  3.58 us (3%)
    pallas_call x1, Pallas kernels, per_device(): pl.pallas_call(functools.partial(kernel, sizes), out_shape=jax.ShapeDtype...  115 us
    unnamed x10, local copies, waits for them, and re-layouts  3.58 us

commit v1 on v0

v1 whole, which is shorter than its diff:
```python
import functools
import math

import jax
import jax.numpy as jnp
from jax import lax
from jax.experimental import pallas as pl
from jax.experimental.pallas import tpu as pltpu
from jax.sharding import PartitionSpec as P

MESH = pl.DeviceIdType.MESH
F32 = jnp.float32
BF16 = jnp.bfloat16
IN_SPACE = pltpu.HBM

Z_HALVES = 2
X_CHIPS = 4


def gate_entries(angle, flag):
    cos_part, sin_part = jnp.cos(angle), jnp.sin(angle)
    weight = flag.astype(F32)
    root = math.sqrt(0.5)
    stay, mix, turn = 1.0 - weight + weight * root, weight * root, 1.0 - weight - weight * root
    return (
        cos_part * stay - sin_part * mix,
        cos_part * mix - sin_part * turn,
        sin_part * stay + cos_part * mix,
        sin_part * mix + cos_part * turn,
    )


def split(value):
    high = value.astype(BF16)
    return high, (value - high.astype(F32)).astype(BF16)


def dot3(left, right):
    dot = functools.partial(jnp.dot, preferred_element_type=F32)
    return dot(left[0], right[0]) + (dot(left[0], right[1]) + dot(left[1], right[0]))


def log2(value):
    return value.bit_length() - 1


def kernel(
    sizes,
    amp_in, angles_in, flags_in, pairs_in, out,
    send_z, recv_z, send_p, recv_p, send_b, recv_b,
    gk, gm, gm_end, gab, sign_mid, sign_end, mid,
    amp, angles, flags, entries, gates, pairs, send_sem, recv_sem, load_sem,
):
    zh, zl, xc, yc, halves, ex, kk = sizes
    nz, np_, nb, na = zh * zl, xc * yc, xc * zl, zh * yc
    mm = halves * zl * ex * xc
    nab = na * nb
    bits_a, bits_b, bits_x, bits_m, bits_k = log2(na), log2(nb), log2(na), log2(mm), log2(kk)
    qubits = bits_a + bits_b + bits_x + bits_m + bits_k
    shift_m = bits_k
    shift_x = shift_m + bits_m
    shift_b = shift_x + bits_x
    shift_a = shift_b + bits_b
    rot_m = bits_a + bits_b
    rot_k = rot_m + bits_m
    sub = ex * xc
    together = 4
    steps = yc // together if yc > together else 1
    together = yc // steps

    me_a, me_b = lax.axis_index("qa"), lax.axis_index("qb")
    my_zh, my_yc = lax.div(me_a, yc), lax.rem(me_a, yc)
    my_x, my_zl = lax.div(me_b, zl), lax.rem(me_b, zl)
    my_z = my_zh * zl + my_zl
    my_p = my_x * yc + my_yc

    def at_z(other, step):
        z_half = lax.rem(my_zh + other, zh)
        z_low = lax.rem(my_zl + step, zl)
        return z_half * zl + z_low, (z_half * yc + my_yc, my_x * zl + z_low)

    def at_p(step):
        p = lax.rem(my_p + step, np_)
        return p, (my_zh * yc + lax.rem(p, yc), lax.div(p, yc) * zl + my_zl)

    run = zl // 2

    def at_b(other, step):
        side = lax.rem(lax.div(my_zl, run) + other, 2)
        place = side * run + lax.rem(my_zl + step, run)
        b = lax.rem(my_x + lax.div(step, run), xc) * zl + place
        return b, (me_a, b)

    def load(number, source, target):
        return pltpu.make_async_copy(source, target, load_sem.at[number])

    small = [load(0, angles_in, angles), load(1, flags_in, flags), load(2, pairs_in, pairs)]
    for copy in small:
        copy.start()

    def amp_part(number):
        z_half = lax.rem(my_zh + 1 + number // steps, zh)
        first = z_half * yc + number % steps * together
        part = pl.ds(first, together)
        return z_half, first, load(3 + number, amp_in.at[part], amp.at[part])

    for number in range(zh * steps):
        amp_part(number)[2].start()

    barrier = pltpu.get_barrier_semaphore()

    def signal(device):
        pl.semaphore_signal(barrier, inc=1, device_id=device, device_id_type=MESH)

    for other in (1, 0):
        pl.loop(1 - other, zl)(lambda step, other=other: signal(at_z(other, step)[1]))
    for other in (1, 0):
        pl.loop(1 - other, nb // 2)(lambda step, other=other: signal(at_b(other, step)[1]))
    pl.loop(1, np_)(lambda step: signal(at_p(step)[1]))

    small[0].wait()
    small[1].wait()
    for number, value in enumerate(gate_entries(angles[...], flags[...])):
        entries[number] = value
    to_scalars = load(0, entries, gates)
    to_scalars.start()
    small[2].wait()
    to_scalars.wait()

    def entry(layer, qubit, out_one, in_one):
        value = lambda number: gates[number, layer, qubit]
        return jnp.where(
            out_one,
            jnp.where(in_one, value(3), value(2)),
            jnp.where(in_one, value(1), value(0)),
        )

    def matrix(layer, out_index, in_index, qubits_and_bits):
        result = None
        for qubit, out_bit, in_bit in qubits_and_bits:
            factor = entry(
                layer, qubit, (out_index & (1 << out_bit)) != 0, (in_index & (1 << in_bit)) != 0
            )
            result = factor if result is None else result * factor
        return result

    def signs(layer, index):
        odd = jnp.zeros(index.shape, jnp.int32)
        for pair in range(pairs.shape[2]):
            mask = jnp.left_shift(1, qubits - 1 - pairs[layer, 0, pair]) | jnp.left_shift(
                1, qubits - 1 - pairs[layer, 1, pair]
            )
            odd = odd ^ jnp.where((index & mask) == mask, 1, 0)
        return 1.0 - 2.0 * odd.astype(F32)

    def build_k(layer):
        rows = lax.broadcasted_iota(jnp.int32, (kk, kk), 0)
        cols = lax.broadcasted_iota(jnp.int32, (kk, kk), 1)
        bits = [(rot_k + n, bits_k - 1 - n, bits_k - 1 - n) for n in range(bits_k)]
        gk[layer, 0], gk[layer, 1] = split(matrix(layer, cols, rows, bits))

    bits_zl, bits_xc, bits_ex, bits_h = log2(zl), log2(xc), log2(ex), log2(halves)

    natural = [bits_m - 1 - n for n in range(bits_m)]

    def build_m():
        rows = lax.broadcasted_iota(jnp.int32, (mm, mm), 0)
        cols = lax.broadcasted_iota(jnp.int32, (mm, mm), 1)
        bits = [(rot_m + n, natural[n], natural[n]) for n in range(bits_m)]
        gm[0], gm[1] = split(matrix(0, rows, cols, bits))

    def build_m_end():
        columns = mm // halves
        rows = lax.broadcasted_iota(jnp.int32, (mm, columns), 0)
        in_bits = (
            natural[:bits_h]
            + [bits_zl - 1 - n for n in range(bits_zl)]
            + [bits_zl + bits_xc + bits_ex - 1 - n for n in range(bits_ex)]
            + [bits_zl + bits_xc - 1 - n for n in range(bits_xc)]
        )
        bits = [(rot_m + n, natural[n], in_bits[n]) for n in range(bits_m)]
        for half in range(halves):
            cols = lax.broadcasted_iota(jnp.int32, (mm, columns), 1) + half * columns
            gm_end[half, 0], gm_end[half, 1] = split(matrix(1, rows, cols, bits))

    bits_yc, bits_zh = log2(yc), log2(zh)

    def mid_bits():
        a_bits = [bits_zl + bits_zh - 1 - n for n in range(bits_zh)]
        a_bits += [bits_zl + bits_zh + bits_yc - 1 - n for n in range(bits_yc)]
        b_bits = [bits_zl + bits_zh + bits_yc + bits_xc - 1 - n for n in range(bits_xc)]
        b_bits += [bits_zl - 1 - n for n in range(bits_zl)]
        return a_bits + b_bits

    tile = min(nab, 64)

    def build_ab(layer):
        mids = mid_bits()
        if layer == 0:
            outs = mids
        else:
            outs = [bits_a - 1 - n for n in range(bits_a)]
            outs += [bits_a + bits_b - 1 - n for n in range(bits_b)]
        bits = [(n, outs[n], mids[n]) for n in range(bits_a + bits_b)]

        @pl.loop(0, nab // tile)
        def _(step):
            start = pl.multiple_of(step * tile, tile)
            rows = lax.broadcasted_iota(jnp.int32, (tile, nab), 0) + start
            cols = lax.broadcasted_iota(jnp.int32, (tile, nab), 1)
            high, low = split(matrix(layer, rows, cols, bits))
            gab[layer, 0, pl.ds(start, tile), :] = high
            gab[layer, 1, pl.ds(start, tile), :] = low

    sign_tile = min(nab, 128)

    def build_sign_mid():
        mids = mid_bits()
        per = nab // sign_tile

        @pl.loop(0, halves * ex * per)
        def _(step):
            part, start = lax.div(step, per), pl.multiple_of(lax.rem(step, per) * sign_tile, sign_tile)
            half, extra = lax.div(part, ex), lax.rem(part, ex)
            rows = lax.broadcasted_iota(jnp.int32, (sign_tile, kk), 0) + start
            cols = lax.broadcasted_iota(jnp.int32, (sign_tile, kk), 1)
            index = cols
            for n in range(bits_a + bits_b):
                index = index | (((rows >> mids[n]) & 1) << (qubits - 1 - n))
            m = ((half * zl + my_zl) * ex + extra) * xc + my_x
            index = index + (m * (1 << shift_m) + me_a * (1 << shift_x))
            sign_mid[half, pl.ds(start, sign_tile), pl.ds(pl.multiple_of(extra * kk, kk), kk)] = signs(0, index)

    def build_sign_end():
        @pl.loop(0, na)
        def _(a):
            rows = lax.broadcasted_iota(jnp.int32, (mm, kk), 0)
            cols = lax.broadcasted_iota(jnp.int32, (mm, kk), 1)
            index = cols + rows * (1 << shift_m)
            index = index + (me_a * (1 << shift_x) + me_b * (1 << shift_b) + a * (1 << shift_a))
            sign_end[a] = signs(1, index)

    def beside(value, rows):
        parts = [value[n * rows : (n + 1) * rows] for n in range(together)]
        return jnp.concatenate(parts, axis=1)

    def layer_0(number):
        z_half, first, copy = amp_part(number)
        copy.wait()
        block = amp[pl.ds(first, together)].reshape(together * mm, kk)
        block = dot3(split(block), (gk[0, 0], gk[0, 1]))
        high, low = split(block)
        block = dot3((gm[0], gm[1]), (beside(high, mm), beside(low, mm)))
        for n in range(together):
            done = block[:, n * kk : (n + 1) * kk].reshape(halves, zl, sub, kk)
            send_z[:, pl.ds(z_half * zl, zl), number % steps * together + n] = done

    def send(source, target, sems, device):
        pltpu.make_async_remote_copy(
            src_ref=source,
            dst_ref=target,
            send_sem=send_sem.at[sems],
            recv_sem=recv_sem.at[sems],
            device_id=device,
            device_id_type=MESH,
        ).start()

    def keep(source, target, sems):
        pltpu.make_async_copy(source, target, recv_sem.at[sems]).start()

    def wait_all(target, sems):
        pltpu.make_async_copy(target, target, recv_sem.at[sems]).wait()

    def wait_sent(part, sems):
        pltpu.make_async_copy(part, part, send_sem.at[sems]).wait()

    def send_z_part(half, other):
        @pl.loop(1 - other, zl)
        def _(step):
            number, device = at_z(other, step)
            send(send_z.at[half, number], recv_z.at[half, my_z], half, device)

    def keep_z(half):
        keep(send_z.at[half, my_z], recv_z.at[half, my_z], half)

    def send_p_half(half):
        @pl.loop(1, np_)
        def _(step):
            number, device = at_p(step)
            send(send_p.at[half, number], recv_p.at[half, my_p], 2 + half, device)

        keep(send_p.at[half, my_p], recv_p.at[half, my_p], 2 + half)

    def b_part(ref, half, number, group):
        return ref.at[half, number] if half == 0 else ref.at[half, number, group]

    def b_parts(half):
        return [(0, 4)] if half == 0 else [(group, 5 + group) for group in range(zh)]

    def send_b_half(half):
        for group, sems in b_parts(half):
            for other in (1, 0):
                @pl.loop(1 - other, nb // 2)
                def _(step):
                    number, device = at_b(other, step)
                    send(b_part(send_b, half, number, group), b_part(recv_b, half, me_b, group), sems, device)

            keep(b_part(send_b, half, me_b, group), b_part(recv_b, half, me_b, group), sems)

    build_k(0)
    build_m()
    for number in range(steps):
        layer_0(number)
    pl.semaphore_wait(barrier, nz + np_ + nb - 3)
    send_z_part(0, 1)
    for number in range(steps, zh * steps):
        layer_0(number)
    send_z_part(0, 0)
    keep_z(0)
    send_z_part(1, 1)
    send_z_part(1, 0)
    keep_z(1)

    build_ab(0)
    build_ab(1)
    build_sign_mid()
    mid_tile = min(nab, 128)

    def middle(half):
        wait_all(recv_z.at[half], half)

        @pl.loop(0, yc)
        def _(xr):
            for z_half in range(zh):
                for low in range(sub):
                    rows = recv_z[half, pl.ds(z_half * zl, zl), xr, low, :]
                    extra, x = low // xc, low % xc
                    send_p[half, x * yc + xr, pl.ds((extra * zh + z_half) * zl, zl), :] = rows

        send_p_half(half)
        wait_all(recv_p.at[half], 2 + half)
        parts = []
        for extra in range(ex):
            part = recv_p[half, :, pl.ds(extra * zh * zl, zh * zl), :]
            parts.append(part.reshape(nab, kk))
        high, low = split(jnp.concatenate(parts, axis=1))
        mid[0, 0] = high
        mid[0, 1] = low

        @pl.loop(0, nab // mid_tile)
        def _(step):
            start = pl.multiple_of(step * mid_tile, mid_tile)
            left = (gab[0, 0, pl.ds(start, mid_tile), :], gab[0, 1, pl.ds(start, mid_tile), :])
            value = dot3(left, (mid[0, 0], mid[0, 1])) * sign_mid[half, pl.ds(start, mid_tile), :]
            high, low = split(value)
            mid[1, 0, pl.ds(start, mid_tile), :] = high
            mid[1, 1, pl.ds(start, mid_tile), :] = low

        @pl.loop(0, nab // mid_tile)
        def _(step):
            start = pl.multiple_of(step * mid_tile, mid_tile)
            left = (gab[1, 0, pl.ds(start, mid_tile), :], gab[1, 1, pl.ds(start, mid_tile), :])
            value = dot3(left, (mid[1, 0], mid[1, 1]))
            places = mid_tile // na
            for extra in range(ex):
                part = value[:, extra * kk : (extra + 1) * kk].reshape(places, zh, yc, kk)
                send_b[half, pl.ds(step * places, places), :, pl.ds(extra * yc, yc), :] = part

        send_b_half(half)

    def last_layer(half, group):
        @pl.loop(0, steps)
        def _(step):
            parts = []
            for n in range(together):
                for extra in range(ex):
                    for x in range(xc):
                        row = extra * yc + step * together + n
                        parts.append(recv_b[half, pl.ds(x * zl, zl), group, row, :])
            block = jnp.concatenate(parts, axis=0)
            block = dot3(split(block), (gk[1, 0], gk[1, 1]))
            high, low = split(block)
            rows = mm // halves
            block = dot3((gm_end[half, 0], gm_end[half, 1]), (beside(high, rows), beside(low, rows)))
            for n in range(together):
                a = group * yc + step * together + n
                value = block[:, n * kk : (n + 1) * kk]
                out[a] = value if half == 0 else (out[a] + value) * sign_end[a]

    for half in range(halves):
        middle(half)
    build_k(1)
    build_m_end()
    build_sign_end()
    wait_all(recv_b.at[0], 4)
    for group in range(zh):
        last_layer(0, group)
    for group, sems in b_parts(1):
        wait_all(recv_b.at[1, :, group], sems)
        last_layer(1, group)

    for half in range(halves):
        wait_sent(send_z.at[half, pl.ds(0, nz - 1)], half)
        wait_sent(send_p.at[half, pl.ds(0, np_ - 1)], 2 + half)
    wait_sent(send_b.at[0, pl.ds(0, nb - 1)], 4)
    for group, sems in b_parts(1):
        wait_sent(send_b.at[1, pl.ds(0, nb - 1), group], sems)


def per_device(amplitudes, angles, hadamard, cz_pairs):
    count_a, count_b = lax.axis_size("qa"), lax.axis_size("qb")
    x_total, mm, kk = amplitudes.shape[2:]
    zh, xc = Z_HALVES, X_CHIPS
    yc, zl = count_a // zh, count_b // xc
    halves = 2
    ex = mm // (halves * zl * xc)
    sizes = (zh, zl, xc, yc, halves, ex, kk)
    nab = count_a * count_b
    layers, rotated = angles.shape
    pairs = cz_pairs.shape[1]
    shape_z = (halves, zh * zl, yc, ex * xc, kk)
    shape_p = (halves, xc * yc, ex * zh * zl, kk)
    shape_b = (halves, xc * zl, zh, ex * yc, kk)
    result = pl.pallas_call(
        functools.partial(kernel, sizes),
        out_shape=jax.ShapeDtypeStruct((count_a, mm, kk), F32),
        in_specs=[pl.BlockSpec(memory_space=IN_SPACE)] * 4,
        out_specs=pl.BlockSpec(memory_space=pltpu.VMEM),
        scratch_shapes=[
            pltpu.VMEM(shape_z, F32),
            pltpu.VMEM(shape_z, F32),
            pltpu.VMEM(shape_p, F32),
            pltpu.VMEM(shape_p, F32),
            pltpu.VMEM(shape_b, F32),
            pltpu.VMEM(shape_b, F32),
            pltpu.VMEM((2, 2, kk, kk), BF16),
            pltpu.VMEM((2, mm, mm), BF16),
            pltpu.VMEM((halves, 2, mm, mm // halves), BF16),
            pltpu.VMEM((2, 2, nab, nab), BF16),
            pltpu.VMEM((halves, nab, ex * kk), F32),
            pltpu.VMEM((count_a, mm, kk), F32),
            pltpu.VMEM((2, 2, nab, ex * kk), BF16),
            pltpu.VMEM((x_total, mm, kk), F32),
            pltpu.VMEM((layers, rotated), F32),
            pltpu.VMEM((layers, rotated), jnp.int32),
            pltpu.VMEM((4, layers, rotated), F32),
            pltpu.SMEM((4, layers, rotated), F32),
            pltpu.SMEM((layers, 2, pairs), jnp.int32),
            pltpu.SemaphoreType.DMA((5 + zh,)),
            pltpu.SemaphoreType.DMA((5 + zh,)),
            pltpu.SemaphoreType.DMA((7,)),
        ],
        compiler_params=pltpu.CompilerParams(
            collective_id=0, has_side_effects=True, vmem_limit_bytes=52 * 2**20
        ),
    )(
        amplitudes.reshape(x_total, mm, kk),
        angles,
        hadamard,
        jnp.transpose(cz_pairs, (0, 2, 1)),
    )
    return result.reshape(1, 1, count_a, mm, kk)


def solution(mesh):
    return jax.shard_map(
        per_device,
        mesh=mesh,
        in_specs=(P("qa", "qb", None, None, None), P(), P(), P()),
        out_specs=P("qa", "qb", None, None, None),
        check_vma=False,
    )
```

time: 119 us -> 113 us (0.950)
  Pallas kernels: 115 us -> 110 us
  local copies, waits for them, and re-layouts: 3.58 us -> 2.34 us
    pallas_call x1, Pallas kernels: 115 us -> 110 us  [per_device(): pl.pallas_call(functools.partial(kernel, sizes), out_shape=jax.ShapeDtype...]
    unnamed x10 -> x7, local copies, waits for them, and re-layouts: 3.58 us -> 2.34 us
where the time goes in v1:
time: 113 us
  Pallas kernels  110 us (97%)
  local copies, waits for them, and re-layouts  2.34 us (2%)
    pallas_call x1, Pallas kernels, per_device(): pl.pallas_call(functools.partial(kernel, sizes), out_shape=jax.ShapeDtype...  110 us
    unnamed x7, local copies, waits for them, and re-layouts  2.34 us

profile of v1, /device:TPU:1, one launch (start us, length us, event | category | flops | bytes accessed | tf_op | source)
XLA Modules:
  0.0 112.6 jit_solution(14611893048031290407)
XLA Ops:
  0.0 0.0 copy-start
  0.0 0.0 copy-start.1
  0.0 0.7 copy-done
  0.7 0.0 copy-done.1
  0.7 0.0 copy-start.2
  0.7 0.7 copy-done.2
  1.4 110.2 %shard_map.46 = f32[16,128,128]{2,1,0:T(8,128)S(1)} custom-call(f32[16,128,128]{2,1,0:T(8,128)} %bitcast.5, f32[2,23]{1,0:T(2,128)S(1)} %copy-done.1, s32[2,23]{1,0:T(2,128)S(1)} %copy-done.2, s32[2,2,14]{2,1,0:T(2,128)S(1)} %bitcast.4), custom_call_target="tpu_custom_call" | custom-call | tf_op jit(solution)/shard_map/pallas_call | solution.py:424
  111.6 1.0 copy.6
Async XLA Ops:
  0.0 0.7 copy-start
  0.0 0.7 copy-start.1
  0.7 0.7 copy-start.2

commit v2 on v1

--- a/solution.py
+++ b/solution.py
@@ -11,7 +11,6 @@
 MESH = pl.DeviceIdType.MESH
 F32 = jnp.float32
 BF16 = jnp.bfloat16
-IN_SPACE = pltpu.HBM
 
 Z_HALVES = 2
 X_CHIPS = 4
@@ -91,6 +90,17 @@
         b = lax.rem(my_x + lax.div(step, run), xc) * zl + place
         return b, (me_a, b)
 
+    barrier = pltpu.get_barrier_semaphore()
+
+    def signal(device):
+        pl.semaphore_signal(barrier, inc=1, device_id=device, device_id_type=MESH)
+
+    for other in (1, 0):
+        pl.loop(1 - other, zl)(lambda step, other=other: signal(at_z(other, step)[1]))
+    for other in (1, 0):
+        pl.loop(1 - other, nb // 2)(lambda step, other=other: signal(at_b(other, step)[1]))
+    pl.loop(1, np_)(lambda step: signal(at_p(step)[1]))
+
     def load(number, source, target):
         return pltpu.make_async_copy(source, target, load_sem.at[number])
 
@@ -106,17 +116,6 @@
 
     for number in range(zh * steps):
         amp_part(number)[2].start()
-
-    barrier = pltpu.get_barrier_semaphore()
-
-    def signal(device):
-        pl.semaphore_signal(barrier, inc=1, device_id=device, device_id_type=MESH)
-
-    for other in (1, 0):
-        pl.loop(1 - other, zl)(lambda step, other=other: signal(at_z(other, step)[1]))
-    for other in (1, 0):
-        pl.loop(1 - other, nb // 2)(lambda step, other=other: signal(at_b(other, step)[1]))
-    pl.loop(1, np_)(lambda step: signal(at_p(step)[1]))
 
     small[0].wait()
     small[1].wait()
@@ -424,7 +423,7 @@
     result = pl.pallas_call(
         functools.partial(kernel, sizes),
         out_shape=jax.ShapeDtypeStruct((count_a, mm, kk), F32),
-        in_specs=[pl.BlockSpec(memory_space=IN_SPACE)] * 4,
+        in_specs=[pl.BlockSpec(memory_space=pltpu.HBM)] * 4,
         out_specs=pl.BlockSpec(memory_space=pltpu.VMEM),
         scratch_shapes=[
             pltpu.VMEM(shape_z, F32),
@@ -451,14 +450,17 @@
             pltpu.SemaphoreType.DMA((7,)),
         ],
         compiler_params=pltpu.CompilerParams(
-            collective_id=0, has_side_effects=True, vmem_limit_bytes=52 * 2**20
+            collective_id=0, has_side_effects=True, vmem_limit_bytes=40 * 2**20
         ),
-    )(
-        amplitudes.reshape(x_total, mm, kk),
-        angles,
-        hadamard,
-        jnp.transpose(cz_pairs, (0, 2, 1)),
-    )
+    )(*(
+        pltpu.with_memory_space_constraint(value, pltpu.HBM)
+        for value in (
+            amplitudes.reshape(x_total, mm, kk),
+            angles,
+            hadamard,
+            jnp.transpose(cz_pairs, (0, 2, 1)),
+        )
+    ))
     return result.reshape(1, 1, count_a, mm, kk)
 
 

time: 113 us -> 112 us (level)
  local copies, waits for them, and re-layouts: 2.34 us -> 0.97 us
    unnamed x7 -> x1, local copies, waits for them, and re-layouts: 2.34 us -> 0.97 us
where the time goes in v2:
time: 112 us; the launch traced here: 111 us
  Pallas kernels  110 us (98%)
    pallas_call x1, Pallas kernels, per_device(): pl.pallas_call(functools.partial(kernel, sizes), out_shape=jax.ShapeDtype...  110 us

profile of v2, /device:TPU:1, one launch (start us, length us, event | category | flops | bytes accessed | tf_op | source)
XLA Modules:
  0.0 111.2 jit_solution(7290684949100669041)
XLA Ops:
  0.0 110.2 %shard_map.46 = f32[16,128,128]{2,1,0:T(8,128)S(1)} custom-call(f32[16,128,128]{2,1,0:T(8,128)} %bitcast.4, f32[2,23]{1,0:T(2,128)} %angles_in.1, s32[2,23]{1,0:T(2,128)} %flags_in.1, s32[2,2,14]{2,1,0:T(2,128)} %bitcast.5), custom_call_target="tpu_custom_call" | custom-call | tf_op jit(solution)/shard_map/pallas_call | solution.py:423
  110.2 1.0 copy.6

commit v3 on v2

--- a/solution.py
+++ b/solution.py
@@ -97,8 +97,6 @@
 
     for other in (1, 0):
         pl.loop(1 - other, zl)(lambda step, other=other: signal(at_z(other, step)[1]))
-    for other in (1, 0):
-        pl.loop(1 - other, nb // 2)(lambda step, other=other: signal(at_b(other, step)[1]))
     pl.loop(1, np_)(lambda step: signal(at_p(step)[1]))
 
     def load(number, source, target):
@@ -310,7 +308,7 @@
     build_m()
     for number in range(steps):
         layer_0(number)
-    pl.semaphore_wait(barrier, nz + np_ + nb - 3)
+    pl.semaphore_wait(barrier, nz + np_ - 2)
     send_z_part(0, 1)
     for number in range(steps, zh * steps):
         layer_0(number)

time: 112 us -> 111 us (level)
  no operation moved by 1% of the time
where the time goes in v3:
time: 111 us
  Pallas kernels  110 us (99%)
    pallas_call x1, Pallas kernels, per_device(): pl.pallas_call(functools.partial(kernel, sizes), out_shape=jax.ShapeDtype...  110 us

profile of v3, /device:TPU:1, one launch (start us, length us, event | category | flops | bytes accessed | tf_op | source)
XLA Modules:
  0.0 111.0 jit_solution(5551453463530868602)
XLA Ops:
  0.0 110.1 %shard_map.46 = f32[16,128,128]{2,1,0:T(8,128)S(1)} custom-call(f32[16,128,128]{2,1,0:T(8,128)} %bitcast.4, f32[2,23]{1,0:T(2,128)} %angles_in.1, s32[2,23]{1,0:T(2,128)} %flags_in.1, s32[2,2,14]{2,1,0:T(2,128)} %bitcast.5), custom_call_target="tpu_custom_call" | custom-call | tf_op jit(solution)/shard_map/pallas_call | solution.py:421
  110.1 1.0 copy.6

commit v4 on v3

--- a/solution.py
+++ b/solution.py
@@ -48,7 +48,7 @@
     amp_in, angles_in, flags_in, pairs_in, out,
     send_z, recv_z, send_p, recv_p, send_b, recv_b,
     gk, gm, gm_end, gab, sign_mid, sign_end, mid,
-    amp, angles, flags, entries, gates, pairs, send_sem, recv_sem, load_sem,
+    amp, angles, flags, entries, gates, pairs, send_sem, recv_sem, load_sem, go_z, runs_sem, go_p,
 ):
     zh, zl, xc, yc, halves, ex, kk = sizes
     nz, np_, nb, na = zh * zl, xc * yc, xc * zl, zh * yc
@@ -92,12 +92,19 @@
 
     barrier = pltpu.get_barrier_semaphore()
 
-    def signal(device):
-        pl.semaphore_signal(barrier, inc=1, device_id=device, device_id_type=MESH)
-
-    for other in (1, 0):
-        pl.loop(1 - other, zl)(lambda step, other=other: signal(at_z(other, step)[1]))
-    pl.loop(1, np_)(lambda step: signal(at_p(step)[1]))
+    def signal(device, semaphore=barrier):
+        pl.semaphore_signal(semaphore, inc=1, device_id=device, device_id_type=MESH)
+
+    def to_p(semaphore):
+        pl.loop(1, np_)(lambda step: signal(at_p(step)[1], semaphore))
+
+    def to_other_run(semaphore):
+        pl.loop(0, zl)(lambda step: signal(at_z(1, step)[1], semaphore))
+
+    second = my_zh == 1
+    pl.loop(1, zl)(lambda step: signal(at_z(0, step)[1]))
+    pl.when(jnp.logical_not(second))(lambda: to_other_run(barrier))
+    pl.when(second)(lambda: to_p(barrier))
 
     def load(number, source, target):
         return pltpu.make_async_copy(source, target, load_sem.at[number])
@@ -107,7 +114,7 @@
         copy.start()
 
     def amp_part(number):
-        z_half = lax.rem(my_zh + 1 + number // steps, zh)
+        z_half = number // steps
         first = z_half * yc + number % steps * together
         part = pl.ds(first, together)
         return z_half, first, load(3 + number, amp_in.at[part], amp.at[part])
@@ -308,15 +315,27 @@
     build_m()
     for number in range(steps):
         layer_0(number)
-    pl.semaphore_wait(barrier, nz + np_ - 2)
-    send_z_part(0, 1)
+    pl.semaphore_wait(barrier, zl - 1 + my_zh * (zl + np_ - 1))
+    pl.when(second)(lambda: to_other_run(go_z))
+    send_z_part(0, my_zh)
+    pl.when(second)(lambda: to_p(runs_sem))
     for number in range(steps, zh * steps):
         layer_0(number)
-    send_z_part(0, 0)
+
+    @pl.when(jnp.logical_not(second))
+    def _():
+        pl.semaphore_wait(go_z, zl)
+
+    send_z_part(0, 1 - my_zh)
     keep_z(0)
-    send_z_part(1, 1)
-    send_z_part(1, 0)
+    send_z_part(1, my_zh)
+    send_z_part(1, 1 - my_zh)
     keep_z(1)
+
+    @pl.when(second)
+    def _():
+        pl.semaphore_wait(runs_sem, np_ - 1)
+        signal(at_z(1, 0)[1], go_p)
 
     build_ab(0)
     build_ab(1)
@@ -333,6 +352,11 @@
                     rows = recv_z[half, pl.ds(z_half * zl, zl), xr, low, :]
                     extra, x = low // xc, low % xc
                     send_p[half, x * yc + xr, pl.ds((extra * zh + z_half) * zl, zl), :] = rows
+
+        if half == 0:
+            @pl.when(jnp.logical_not(second))
+            def _():
+                pl.semaphore_wait(go_p, 1)
 
         send_p_half(half)
         wait_all(recv_p.at[half], 2 + half)
@@ -446,6 +470,9 @@
             pltpu.SemaphoreType.DMA((5 + zh,)),
             pltpu.SemaphoreType.DMA((5 + zh,)),
             pltpu.SemaphoreType.DMA((7,)),
+            pltpu.SemaphoreType.REGULAR,
+            pltpu.SemaphoreType.REGULAR,
+            pltpu.SemaphoreType.REGULAR,
         ],
         compiler_params=pltpu.CompilerParams(
             collective_id=0, has_side_effects=True, vmem_limit_bytes=40 * 2**20

time: 111 us -> 107 us (0.964)
  Pallas kernels: 110 us -> 106 us
    pallas_call x1, Pallas kernels: 110 us -> 106 us  [per_device(): pl.pallas_call(functools.partial(kernel, sizes), out_shape=jax.ShapeDtype...]
where the time goes in v4:
time: 107 us
  Pallas kernels  106 us (99%)
    pallas_call x1, Pallas kernels, per_device(): pl.pallas_call(functools.partial(kernel, sizes), out_shape=jax.ShapeDtype...  106 us

profile of v4, /device:TPU:1, one launch (start us, length us, event | category | flops | bytes accessed | tf_op | source)
XLA Modules:
  0.0 107.2 jit_solution(13867267894168978487)
XLA Ops:
  0.0 106.2 %shard_map.46 = f32[16,128,128]{2,1,0:T(8,128)S(1)} custom-call(f32[16,128,128]{2,1,0:T(8,128)} %bitcast.4, f32[2,23]{1,0:T(2,128)} %angles_in.1, s32[2,23]{1,0:T(2,128)} %flags_in.1, s32[2,2,14]{2,1,0:T(2,128)} %bitcast.5), custom_call_target="tpu_custom_call" | custom-call | tf_op jit(solution)/shard_map/pallas_call | solution.py:445
  106.2 1.0 copy.6

commit v5 on v4

--- a/solution.py
+++ b/solution.py
@@ -303,11 +303,10 @@
 
     def send_b_half(half):
         for group, sems in b_parts(half):
-            for other in (1, 0):
-                @pl.loop(1 - other, nb // 2)
-                def _(step):
-                    number, device = at_b(other, step)
-                    send(b_part(send_b, half, number, group), b_part(recv_b, half, me_b, group), sems, device)
+            @pl.loop(1, nb)
+            def _(step):
+                number = lax.rem(me_b + step, nb)
+                send(b_part(send_b, half, number, group), b_part(recv_b, half, me_b, group), sems, (me_a, number))
 
             keep(b_part(send_b, half, me_b, group), b_part(recv_b, half, me_b, group), sems)
 
@@ -324,6 +323,7 @@
 
     @pl.when(jnp.logical_not(second))
     def _():
+        build_ab(0)
         pl.semaphore_wait(go_z, zl)
 
     send_z_part(0, 1 - my_zh)
@@ -337,7 +337,7 @@
         pl.semaphore_wait(runs_sem, np_ - 1)
         signal(at_z(1, 0)[1], go_p)
 
-    build_ab(0)
+    pl.when(second)(lambda: build_ab(0))
     build_ab(1)
     build_sign_mid()
     mid_tile = min(nab, 128)

time: 107 us -> 107 us (level)
  no operation moved by 1% of the time
where the time goes in v5:
time: 107 us; the launch traced here: 106 us
  Pallas kernels  105 us (98%)
    pallas_call x1, Pallas kernels, per_device(): pl.pallas_call(functools.partial(kernel, sizes), out_shape=jax.ShapeDtype...  105 us

profile of v5, /device:TPU:1, one launch (start us, length us, event | category | flops | bytes accessed | tf_op | source)
XLA Modules:
  0.0 106.5 jit_solution(1384187683758147128)
XLA Ops:
  0.0 105.5 %shard_map.46 = f32[16,128,128]{2,1,0:T(8,128)S(1)} custom-call(f32[16,128,128]{2,1,0:T(8,128)} %bitcast.4, f32[2,23]{1,0:T(2,128)} %angles_in.1, s32[2,23]{1,0:T(2,128)} %flags_in.1, s32[2,2,14]{2,1,0:T(2,128)} %bitcast.5), custom_call_target="tpu_custom_call" | custom-call | tf_op jit(solution)/shard_map/pallas_call | solution.py:445
  105.5 1.0 copy.6

commit v6 on v5

--- a/solution.py
+++ b/solution.py
@@ -75,11 +75,11 @@
 
     def at_z(other, step):
         z_half = lax.rem(my_zh + other, zh)
-        z_low = lax.rem(my_zl + step, zl)
+        z_low = lax.rem(my_zl + zl - step, zl)
         return z_half * zl + z_low, (z_half * yc + my_yc, my_x * zl + z_low)
 
     def at_p(step):
-        p = lax.rem(my_p + step, np_)
+        p = lax.rem(my_p + 5 * step, np_)
         return p, (my_zh * yc + lax.rem(p, yc), lax.div(p, yc) * zl + my_zl)
 
     run = zl // 2
@@ -390,7 +390,7 @@
         send_b_half(half)
 
     def last_layer(half, group):
-        @pl.loop(0, steps)
+        @pl.loop(0, steps, unroll=True)
         def _(step):
             parts = []
             for n in range(together):

time: 107 us -> 106 us (level)
  no operation moved by 1% of the time
where the time goes in v6:
time: 106 us
  Pallas kernels  105 us (99%)
    pallas_call x1, Pallas kernels, per_device(): pl.pallas_call(functools.partial(kernel, sizes), out_shape=jax.ShapeDtype...  105 us

profile of v6, /device:TPU:1, one launch (start us, length us, event | category | flops | bytes accessed | tf_op | source)
XLA Modules:
  0.0 105.7 jit_solution(7141097479197701207)
XLA Ops:
  0.0 104.7 %shard_map.46 = f32[16,128,128]{2,1,0:T(8,128)S(1)} custom-call(f32[16,128,128]{2,1,0:T(8,128)} %bitcast.4, f32[2,23]{1,0:T(2,128)} %angles_in.1, s32[2,23]{1,0:T(2,128)} %flags_in.1, s32[2,2,14]{2,1,0:T(2,128)} %bitcast.5), custom_call_target="tpu_custom_call" | custom-call | tf_op jit(solution)/shard_map/pallas_call | solution.py:445
  104.7 1.0 copy.6

commit v7 on v6

--- a/solution.py
+++ b/solution.py
@@ -416,14 +416,14 @@
     wait_all(recv_b.at[0], 4)
     for group in range(zh):
         last_layer(0, group)
-    for group, sems in b_parts(1):
-        wait_all(recv_b.at[1, :, group], sems)
-        last_layer(1, group)
-
     for half in range(halves):
         wait_sent(send_z.at[half, pl.ds(0, nz - 1)], half)
         wait_sent(send_p.at[half, pl.ds(0, np_ - 1)], 2 + half)
     wait_sent(send_b.at[0, pl.ds(0, nb - 1)], 4)
+    for group, sems in b_parts(1):
+        wait_all(recv_b.at[1, :, group], sems)
+        last_layer(1, group)
+
     for group, sems in b_parts(1):
         wait_sent(send_b.at[1, pl.ds(0, nb - 1), group], sems)
 

time: 106 us -> 106 us (level)
  no operation moved by 1% of the time
where the time goes in v7:
time: 106 us
  Pallas kernels  105 us (99%)
    pallas_call x1, Pallas kernels, per_device(): pl.pallas_call(functools.partial(kernel, sizes), out_shape=jax.ShapeDtype...  105 us

profile of v7, /device:TPU:1, one launch (start us, length us, event | category | flops | bytes accessed | tf_op | source)
XLA Modules:
  0.0 105.7 jit_solution(11251004903778962040)
XLA Ops:
  0.0 104.7 %shard_map.46 = f32[16,128,128]{2,1,0:T(8,128)S(1)} custom-call(f32[16,128,128]{2,1,0:T(8,128)} %bitcast.4, f32[2,23]{1,0:T(2,128)} %angles_in.1, s32[2,23]{1,0:T(2,128)} %flags_in.1, s32[2,2,14]{2,1,0:T(2,128)} %bitcast.5), custom_call_target="tpu_custom_call" | custom-call | tf_op jit(solution)/shard_map/pallas_call | solution.py:445
  104.7 1.0 copy.6
